TPU v7x, 32 devices: a whole 2x2x4 slice. The times are simulated.
32 devices in a mesh: replica: 8 (over z, x), expert: 4 (over y, core).
Axes of the slice: x: 2, y: 2, z: 4, core: 2. Of those that a mesh axis runs over, the one named last changes fastest.
Arguments:
- master: float32 [8, 4, 4, 64, 768], P('replica', 'expert'), may hold values from -6 to 6
- first_moment: float32 [8, 4, 4, 64, 768], P('replica', 'expert'), may hold values from -4 to 4
- second_moment: float32 [8, 4, 4, 64, 768], P('replica', 'expert'), may hold values from 0.001 to 1
- gradient: bfloat16 [8, 4, 4, 64, 768], P('replica', 'expert'), may hold values from -6 to 6
- scale_exponent: int32 [8, 4, 4, 64, 6], P('replica', 'expert'), may hold values from 3 to 7
- slot_expert: int32 [8, 4, 4], P('replica', 'expert'), may hold values from 0 to 3, each once within a row
- expert_owner: int32 [4], replicated, may hold values from 0 to 3, each once
- serving_weights: bfloat16 [4, 2048, 768], P('expert'), may hold values from -6 to 6
Outputs:
- master_out: float32 [8, 4, 4, 64, 768], P('replica', 'expert')
- first_out: float32 [8, 4, 4, 64, 768], P('replica', 'expert')
- second_out: float32 [8, 4, 4, 64, 768], P('replica', 'expert')
- serving_out: bfloat16 [4, 2048, 768], P('expert')
Inputs may be any that keep to these rules, and one draw needn't show every extreme that they name: `slot_expert`: each row along the last dimension names every expert once. `expert_owner`: names every owner once.
All inputs are finite; a program needn't handle non-finite values.
Results may differ from a plain program's by a relative error of at most 0.0015.
Values may be sent and summed in bfloat16 or wider, within the bound.
A program may use at most 64 MiB of HBM per device.

v0:
```python
import jax
import jax.numpy as jnp
from jax import lax
from jax.sharding import PartitionSpec as P


def apply_rows(serving_rows, coded_rows, scale_rows):
    count = coded_rows.shape[0]
    blocks = scale_rows.shape[1]
    shaped = coded_rows.reshape(count, blocks, -1).astype(jnp.float32)
    added = (shaped * scale_rows.astype(jnp.float32)[..., None]).reshape(count, -1)
    return (serving_rows.astype(jnp.float32) + added).astype(jnp.bfloat16)


def shards(
    master,
    first_moment,
    second_moment,
    gradient,
    scale_exponent,
    slot_expert,
    expert_owner,
    serving_weights,
):
    grad_full = gradient.astype(jnp.float32)
    first_out = 0.9 * first_moment + 0.1 * grad_full
    second_out = 0.95 * second_moment + 0.05 * grad_full * grad_full
    corr_first = 1.0 - 0.9**10
    corr_second = 1.0 - 0.95**10
    update = first_out / corr_first / (jnp.sqrt(second_out / corr_second) + 1e-08) + 0.1 * master
    delta = -0.1 * update
    master_out = master + delta
    slots = master.shape[2]
    sub_rows = master.shape[3]
    columns = master.shape[4]
    blocks = scale_exponent.shape[4]
    scale = jnp.exp2(-scale_exponent[0, 0].astype(jnp.float32))
    shaped = delta[0, 0].reshape(slots, sub_rows, blocks, columns // blocks)
    coded = (
        jnp.clip(shaped / scale[..., None], -8.0, 8.0)
        .astype(jnp.bfloat16)
        .reshape(slots, sub_rows, columns)
    )
    scale_wire = scale.astype(jnp.bfloat16)
    target = expert_owner[slot_expert[0, 0]]
    ordering = jnp.zeros((slots,), jnp.int32).at[target].set(jnp.arange(slots, dtype=jnp.int32))
    coded_sent = coded[ordering]
    scale_sent = scale_wire[ordering]
    coded_recv = lax.all_to_all(coded_sent, "expert", split_axis=0, concat_axis=0, tiled=True)
    scale_recv = lax.all_to_all(scale_sent, "expert", split_axis=0, concat_axis=0, tiled=True)
    piece_rows = slots * sub_rows
    coded_piece = coded_recv.reshape(piece_rows, columns)
    scale_piece = scale_recv.reshape(piece_rows, blocks)
    serving_flat = serving_weights[0]
    new_rows = apply_rows(
        serving_flat,
        lax.all_gather(coded_piece, "replica", axis=0, tiled=True),
        lax.all_gather(scale_piece, "replica", axis=0, tiled=True),
    )
    return (master_out, first_out, second_out, new_rows[None])


def solution(mesh):
    in_specs = (
        P("replica", "expert", None, None, None),
        P("replica", "expert", None, None, None),
        P("replica", "expert", None, None, None),
        P("replica", "expert", None, None, None),
        P("replica", "expert", None, None, None),
        P("replica", "expert", None),
        P(),
        P("expert", None, None),
    )
    out_specs = (
        P("replica", "expert", None, None, None),
        P("replica", "expert", None, None, None),
        P("replica", "expert", None, None, None),
        P("expert", None, None),
    )
    return jax.shard_map(shards, mesh=mesh, in_specs=in_specs, out_specs=out_specs, check_vma=False)
```

profile of v0, /device:TPU:0, one launch (start us, length us, event | category | flops | bytes accessed | tf_op | source)
XLA Modules:
  0.0 108.0 jit_solution(17431260710399105142)
XLA Ops:
  7.2 0.0 copy-start
  7.2 0.0 copy-start.1
  7.2 0.0 all-gather.2.cloned.1.call-start
  7.2 0.7 fusion.9
  8.0 0.0 copy-done
  8.0 0.6 gather_fusion
  8.6 0.6 scatter_custom_fusion
  9.2 0.7 fusion.13
  10.0 0.1 copy.21
  10.1 0.3 div.31
  10.4 0.2 div.32
  10.6 0.0 copy-done.1
  10.6 2.9 %fusion.4 = (bf16[4,64,768]{2,1,0:T(8,128)(2,1)}, f32[1,1,4,64,768]{4,3,2,1,0:T(8,128)S(1)}, f32[1,1,4,64,768]{4,3,2,1,0:T(8,128)S(1)}) fusion(f32[4,64,768]{2,1,0:T(8,128)S(1)} %div.32, f32[1,1,4,64,768]{4,3,2,1,0:T(8,128)S(1)} %copy-done.1, bf16[1,1,4,64,768]{4,3,2,1,0:T(8,128)(2,1)} %param.11, f32[1,1,4,64,768]{4,3,2,1,0:T(8,128)} %param.9, ...), kind=kLoop, calls=%fused_computation.13 | loop fusion | flops 3538944 | bytes 5505024 | tf_op jit(solution)/shard_map/convert_element_type | solution.py:41
  13.6 0.0 copy-start.2
  13.6 0.0 copy-start.3
  13.6 1.8 %gather_fusion.1 = bf16[4,64,768]{2,1,0:T(8,128)(2,1)S(1)} fusion(bf16[4,64,768]{2,1,0:T(8,128)(2,1)} %get-tuple-element.12, s32[1024]{0:T(1024)S(1)} %pad_clamp_fusion), kind=kCustom, calls=%fused_computation.1 | custom fusion | bytes 786448 | tf_op jit(solution)/shard_map/gather | solution.py:47
  15.4 11.5 %all_to_all.10 = bf16[4,64,768]{2,1,0:T(8,128)(2,1)S(1)} all-to-all(bf16[4,64,768]{2,1,0:T(8,128)(2,1)S(1)} %gather_fusion.1), channel_id=1, replica_groups=mesh['replica'=8,'expert'=4] {'expert'}, dimensions={0} | all-to-all | bytes 786432 | tf_op jit(solution)/shard_map/all_to_all | solution.py:49
  26.9 0.9 copy.22
  27.8 0.0 all-gather.2.cloned.1.call-update
  27.8 0.6 gather_fusion.2
  28.4 0.7 reshape.116
  29.1 3.2 %all-to-all-start.1 = ((bf16[4,2,192]{2,1,0:T(2,128)(2,1)}), bf16[4,2,192]{2,1,0:T(2,128)(2,1)S(1)}, u32[]{:S(2)}, u32[]{:S(2)}) async-start(bf16[4,2,192]{2,1,0:T(2,128)(2,1)} %reshape.116), calls=%async_computation.1 | async-start | bytes 8192 | tf_op jit(solution)/shard_map/all_to_all | solution.py:50
  32.3 0.0 copy-done.2
  32.3 0.0 copy-done.3
  32.3 1.3 %fusion.14 = f32[1,1,4,64,768]{4,3,2,1,0:T(8,128)} fusion(f32[1,1,4,64,768]{4,3,2,1,0:T(8,128)S(1)} %copy-done.1, f32[1,1,4,64,768]{4,3,2,1,0:T(8,128)S(1)} %get-tuple-element.14, f32[1,1,4,64,768]{4,3,2,1,0:T(8,128)S(1)} %get-tuple-element.13), kind=kLoop, calls=%fused_computation.30 | loop fusion | flops 1572864 | bytes 3145728 | tf_op jit(solution)/shard_map/add | solution.py:32
  33.6 3.2 %copy.19 = bf16[1,2048,768]{1,2,0:T(8,128)(2,1)S(1)} copy(bf16[1,2048,768]{2,1,0:T(8,128)(2,1)} %param.15) | data formatting | bytes 6291456 | tf_op args[7]
  36.9 0.0 all-to-all-done.1
  36.9 0.1 reshape.117
  37.0 0.1 reshape.78
  37.0 31.2 %all_gather.7 = bf16[2048,6]{0,1:T(8,128)(2,1)S(1)} all-gather(bf16[256,6]{0,1:T(8,128)(2,1)S(1)} %reshape.78), channel_id=1, replica_groups=mesh['replica'=8,'expert'=4] {'replica'}, dimensions={0}, use_global_device_ids=true | all-gather | bytes 27648 | tf_op jit(solution)/shard_map/all_gather | solution.py:58
  68.2 23.3 %all-gather.2.cloned.1.call-done = bf16[2048,768]{0,1:T(8,128)(2,1)} async-done(((bf16[256,768]{0,1:T(8,128)(2,1)}), bf16[2048,768]{0,1:T(8,128)(2,1)}) %all-gather.2.cloned.1.call-update) | async-done | bytes 3145744 | tf_op jit(solution)/shard_map/all_gather | solution.py:57
  91.5 5.0 %fusion = bf16[2048,768]{0,1:T(8,128)(2,1)} fusion(bf16[2048,768]{0,1:T(8,128)(2,1)} %all-gather.2.cloned.1.call-done, bf16[1,2048,768]{1,2,0:T(8,128)(2,1)S(1)} %copy.19, f32[2048,6]{0,1:T(8,128)S(1)} %convert_element_type.41), kind=kLoop, calls=%fused_computation.5 | loop fusion | flops 7864320 | bytes 9486336 | tf_op jit(solution)/shard_map/convert_element_type | solution.py:12
  96.5 4.6 %copy.24 = bf16[1,2048,768]{2,1,0:T(8,128)(2,1)} copy(bf16[1,2048,768]{1,2,0:T(8,128)(2,1)} %bitcast.32) | data formatting | bytes 6291456
  (7 shorter events, 0.0 us)
Async XLA Ops:
  7.2 0.8 copy-start
  7.2 3.4 %copy-start.1 = (f32[1,1,4,64,768]{4,3,2,1,0:T(8,128)S(1)}, f32[1,1,4,64,768]{4,3,2,1,0:T(8,128)}, u32[]{:S(2)}) copy-start(f32[1,1,4,64,768]{4,3,2,1,0:T(8,128)} %param.8) | copy-start | bytes 2359300
  7.2 84.3 %all-gather.2.cloned.1.call-start = ((), (), s32[]{:S(2)}) async-start(), calls=%async_computation.2 | async-start | bytes 3538944 | tf_op jit(solution)/shard_map/all_gather | solution.py:57
  13.6 18.7 %copy-start.2 = (f32[1,1,4,64,768]{4,3,2,1,0:T(8,128)}, f32[1,1,4,64,768]{4,3,2,1,0:T(8,128)S(1)}, u32[]{:S(2)}) copy-start(f32[1,1,4,64,768]{4,3,2,1,0:T(8,128)S(1)} %get-tuple-element.13) | copy-start | bytes 2359300
  13.6 18.7 %copy-start.3 = (f32[1,1,4,64,768]{4,3,2,1,0:T(8,128)}, f32[1,1,4,64,768]{4,3,2,1,0:T(8,128)S(1)}, u32[]{:S(2)}) copy-start(f32[1,1,4,64,768]{4,3,2,1,0:T(8,128)S(1)} %get-tuple-element.14) | copy-start | bytes 2359300
  29.1 7.8 %all-to-all-start.1 = ((bf16[4,2,192]{2,1,0:T(2,128)(2,1)}), bf16[4,2,192]{2,1,0:T(2,128)(2,1)S(1)}, u32[]{:S(2)}, u32[]{:S(2)}) async-start(bf16[4,2,192]{2,1,0:T(2,128)(2,1)} %reshape.116), calls=%async_computation.1 | async-start | bytes 8192 | tf_op jit(solution)/shard_map/all_to_all | solution.py:50
Sparse Core Ops, SparseCore 0:
  27.9 63.5 all-gather.1
where the time goes:
time: 109 us; the launch traced here: 108 us
  blocking collectives  42.7 us (39%)
  waiting for transfers between devices  23.3 us (21%)
  between operations  14.2 us (13%)
  local copies, waits for them, and re-layouts  13.9 us (13%)
  other arithmetic  10.7 us (10%)
  starting transfers between devices  3.26 us (3%)
    all_gather x1, blocking collectives, shards(): lax.all_gather(scale_piece, 'replica', axis=0, tiled=True)  31.2 us
    all_gather x1, waiting for transfers between devices, shards(): lax.all_gather(coded_piece, 'replica', axis=0, tiled=True)  23.3 us
    all_to_all x1, blocking collectives, shards(): lax.all_to_all(coded_sent, 'expert', split_axis=0, concat_axis=0, tiled=T...  11.5 us
    unnamed x12, local copies, waits for them, and re-layouts  8.65 us
    convert_element_type x1, other arithmetic, apply_rows(): return (serving_rows.astype(jnp.float32) + added).astype(jnp.bfloat16)  5.02 us
    all_to_all x1, starting transfers between devices, shards(): lax.all_to_all(scale_sent, 'expert', split_axis=0, concat_axis=0, tiled=T...  3.22 us
    convert_element_type x1, other arithmetic, shards(): coded = jnp.clip(shaped / scale[..., None], -8.0, 8.0).astype(jnp.bfloat1...  2.95 us
  transfers between devices with their start and end apart: 2, of which 1 were waited for; matrix products, arithmetic and copies ran while one was open for 6% of the time, Pallas kernels for 0%

commit v1 on v0

v1 whole, which is shorter than its diff:
```python
import functools

import jax
import jax.numpy as jnp
from jax import lax
from jax.experimental import pallas as pl
from jax.experimental.pallas import tpu as pltpu
from jax.sharding import PartitionSpec as P

MESH = pl.DeviceIdType.MESH
CORES = 2


def adam(master, first_moment, second_moment, gradient):
    grad_full = gradient.astype(jnp.float32)
    first_out = 0.9 * first_moment + 0.1 * grad_full
    second_out = 0.95 * second_moment + 0.05 * grad_full * grad_full
    corr_first = 1.0 - 0.9**10
    corr_second = 1.0 - 0.95**10
    update = first_out / corr_first / (jnp.sqrt(second_out / corr_second) + 1e-08) + 0.1 * master
    delta = -0.1 * update
    return master + delta, first_out, second_out, delta


def adam_kernel(slot_ref, owner_ref, m_ref, f_ref, s_ref, g_ref, e_ref, mo_ref, fo_ref, so_ref, d_ref):
    columns = m_ref.shape[-1]
    blocks = e_ref.shape[-1]
    width = columns // blocks
    limits = jnp.left_shift(1, 7 - e_ref[0]).astype(jnp.float32) * (8.0 / 128.0)
    for b in range(blocks):
        cols = slice(b * width, (b + 1) * width)
        mo, fo, so, delta = adam(m_ref[0, :, cols], f_ref[0, :, cols], s_ref[0, :, cols], g_ref[0, :, cols])
        mo_ref[0, :, cols] = mo
        fo_ref[0, :, cols] = fo
        so_ref[0, :, cols] = so
        limit = limits[:, b : b + 1]
        d_ref[0, :, cols] = jnp.minimum(jnp.maximum(delta, -limit), limit).astype(jnp.bfloat16)


def local_step(slot_expert, expert_owner, master, first_moment, second_moment, gradient, scale_exponent):
    slots, rows, columns = master.shape
    blocks = scale_exponent.shape[-1]
    here = pl.BlockSpec((1, rows, columns), lambda s, se, eo: (s, 0, 0))
    small = pl.BlockSpec((1, rows, blocks), lambda s, se, eo: (s, 0, 0))
    owned = pl.BlockSpec((1, rows, columns), lambda s, se, eo: (eo[se[s]], 0, 0))
    flat = jax.ShapeDtypeStruct(master.shape, jnp.float32)
    return pl.pallas_call(
        adam_kernel,
        grid_spec=pltpu.PrefetchScalarGridSpec(
            num_scalar_prefetch=2,
            grid=(slots,),
            in_specs=[here, here, here, here, small],
            out_specs=[here, here, here, owned],
        ),
        out_shape=[flat, flat, flat, jax.ShapeDtypeStruct(master.shape, jnp.bfloat16)],
        name="adam_step",
    )(slot_expert, expert_owner, master, first_moment, second_moment, gradient, scale_exponent)


def ring_position(index, count):
    return (index // 2) * (1 - index % 2) + (count - 1 - index // 2) * (index % 2)


def ring_index(position, count):
    back = position // (count // 2)
    return 2 * position * (1 - back) + (2 * (count - 1 - position) + 1) * back


def exchange_kernel(n_rep, n_exp, d_ref, out_ref, own_sem, p_send, p_recv, r_send, r_recv):
    rep = lax.axis_index("replica")
    exp = lax.axis_index("expert")
    pos = ring_position(rep, n_rep)
    ahead = ring_index((pos + 1) % n_rep, n_rep)
    behind = ring_index((pos + n_rep - 1) % n_rep, n_rep)
    chips = n_exp // CORES
    chip, core = exp // CORES, exp % CORES

    def peer(k, sign):
        dc, dk = k // CORES, k % CORES
        return ((chip + sign * dc + chips) % chips) * CORES + (core + sign * dk + CORES) % CORES

    barrier = pltpu.get_barrier_semaphore()
    for k in range(1, n_exp):
        pl.semaphore_signal(barrier, inc=1, device_id=(rep, peer(k, 1)), device_id_type=MESH)
    for near in (ahead, behind):
        pl.semaphore_signal(barrier, inc=1, device_id=(near, exp), device_id_type=MESH)
    own = pltpu.make_async_copy(d_ref.at[exp], out_ref.at[rep, exp], own_sem)
    own.start()
    pl.semaphore_wait(barrier, n_exp + 1)

    swaps = {}
    for k in list(range(CORES, n_exp)) + list(range(1, CORES)):
        swaps[k] = pltpu.make_async_remote_copy(
            src_ref=d_ref.at[peer(k, 1)],
            dst_ref=out_ref.at[rep, exp],
            send_sem=p_send.at[k],
            recv_sem=p_recv.at[k],
            device_id=(rep, peer(k, 1)),
            device_id_type=MESH,
        )
        swaps[k].start()

    far, near = n_rep // 2, n_rep - 1 - n_rep // 2
    hops = [[far if (k % 4 in (0, 3)) == (way == 0) else near for k in range(n_exp)] for way in (0, 1)]

    def ring(way, h, k):
        step = h if way == 0 else n_rep - h
        origin = ring_index((pos + n_rep - step) % n_rep, n_rep)
        block = out_ref.at[origin, peer(k, -1)]
        return pltpu.make_async_remote_copy(
            src_ref=block,
            dst_ref=block,
            send_sem=r_send.at[way, h, k],
            recv_sem=r_recv.at[way, h, k],
            device_id=(ahead if way == 0 else behind, exp),
            device_id_type=MESH,
        )

    sent = []
    for h in range(far):
        for k in range(n_exp):
            if h == 0:
                if k == 0:
                    own.wait()
                else:
                    swaps[k].wait_recv()
            for way in (0, 1):
                if h and h - 1 < hops[way][k]:
                    ring(way, h - 1, k).wait_recv()
                if h < hops[way][k]:
                    copy = ring(way, h, k)
                    copy.start()
                    sent.append(copy)
    for way in (0, 1):
        for k in range(n_exp):
            if hops[way][k] == far:
                ring(way, far - 1, k).wait_recv()
    for k in range(1, n_exp):
        swaps[k].wait_send()
    for copy in sent:
        copy.wait_send()


def exchange(n_rep, n_exp, delta):
    slots, rows, columns = delta.shape
    size = n_rep * n_exp * rows * columns * 2
    far = n_rep // 2
    return pl.pallas_call(
        functools.partial(exchange_kernel, n_rep, n_exp),
        out_shape=jax.ShapeDtypeStruct((n_rep, n_exp, rows, columns), jnp.bfloat16),
        in_specs=[pl.BlockSpec(memory_space=pltpu.VMEM)],
        out_specs=pl.BlockSpec(memory_space=pltpu.VMEM),
        scratch_shapes=[
            pltpu.SemaphoreType.DMA(()),
            pltpu.SemaphoreType.DMA((n_exp,)),
            pltpu.SemaphoreType.DMA((n_exp,)),
            pltpu.SemaphoreType.DMA((2, far, n_exp)),
            pltpu.SemaphoreType.DMA((2, far, n_exp)),
        ],
        compiler_params=pltpu.CompilerParams(
            collective_id=0, has_side_effects=True, vmem_limit_bytes=24 * 1024 * 1024
        ),
        cost_estimate=pl.CostEstimate(flops=0, bytes_accessed=size, transcendentals=0),
        name="exchange",
    )(delta)


def exchange_by_collectives(delta):
    received = lax.all_to_all(delta, "expert", split_axis=0, concat_axis=0, tiled=True)
    return lax.all_gather(received, "replica", axis=0, tiled=False)


def shards(
    n_rep,
    n_exp,
    master,
    first_moment,
    second_moment,
    gradient,
    scale_exponent,
    slot_expert,
    expert_owner,
    serving_weights,
):
    master_out, first_out, second_out, delta = local_step(
        slot_expert[0, 0],
        expert_owner,
        master[0, 0],
        first_moment[0, 0],
        second_moment[0, 0],
        gradient[0, 0],
        scale_exponent[0, 0],
    )
    rows = master.shape[3]
    if rows % 16 == 0 and n_rep % 2 == 0 and n_exp % CORES == 0:
        gathered = exchange(n_rep, n_exp, delta)
    else:
        gathered = exchange_by_collectives(delta)
    added = gathered.reshape(serving_weights.shape).astype(jnp.float32)
    serving_out = (serving_weights.astype(jnp.float32) + added).astype(jnp.bfloat16)
    return (master_out[None, None], first_out[None, None], second_out[None, None], serving_out)


def solution(mesh):
    flat = P("replica", "expert", None, None, None)
    in_specs = (flat, flat, flat, flat, flat, P("replica", "expert", None), P(), P("expert", None, None))
    out_specs = (flat, flat, flat, P("expert", None, None))
    body = functools.partial(shards, mesh.shape["replica"], mesh.shape["expert"])
    return jax.shard_map(body, mesh=mesh, in_specs=in_specs, out_specs=out_specs, check_vma=False)
```

time: 109 us -> 47.8 us (0.44)
  blocking collectives: 42.7 us -> 0 us
  Pallas kernels: 0 us -> 41.7 us
  waiting for transfers between devices: 23.3 us -> 0 us
  between operations: 14.2 us -> 0.65 us
  local copies, waits for them, and re-layouts: 13.9 us -> 2.47 us
  other arithmetic: 10.7 us -> 2.66 us
  starting transfers between devices: 3.26 us -> 0 us
    pallas_call x0 -> x2, Pallas kernels: none -> 41.7 us  [the longest x1 36.7 us: exchange(): pl.pallas_call(functools.partial(exchange_kernel, n_rep, n_exp), out_shap...]
    all_gather x1 -> x0, blocking collectives: 31.2 us -> none  [shards(): lax.all_gather(scale_piece, 'replica', axis=0, tiled=True)]
    all_gather x1 -> x0, waiting for transfers between devices: 23.3 us -> none  [shards(): lax.all_gather(coded_piece, 'replica', axis=0, tiled=True)]
    all_to_all x1 -> x0, blocking collectives: 11.5 us -> none  [shards(): lax.all_to_all(coded_sent, 'expert', split_axis=0, concat_axis=0, tiled=T...]
    unnamed x12 -> x5, local copies, waits for them, and re-layouts: 8.65 us -> 2.47 us
    convert_element_type x4 -> x1, other arithmetic: 8.7 us -> 2.66 us  [shards(): (serving_weights.astype(jnp.float32) + added).astype(jnp.bfloat16)]
    all_to_all x1 -> x0, starting transfers between devices: 3.22 us -> none  [shards(): lax.all_to_all(scale_sent, 'expert', split_axis=0, concat_axis=0, tiled=T...]
    gather x3 -> x0, local copies, waits for them, and re-layouts: 3.03 us -> none  [the longest x1 1.83 us: shards(): coded_sent = coded[ordering]]
  transfers between devices with their start and end apart: 2 -> 0, of which waited for: 1 -> 0; matrix products, arithmetic and copies ran while one was open for 6% -> 0% of each run, Pallas kernels for 0% -> 0%
where the time goes in v1:
time: 47.8 us; the launch traced here: 47.5 us
  Pallas kernels  41.7 us (87%)
  other arithmetic  2.66 us (6%)
  local copies, waits for them, and re-layouts  2.47 us (5%)
  between operations  0.65 us (1%)
    pallas_call x1, Pallas kernels, exchange(): pl.pallas_call(functools.partial(exchange_kernel, n_rep, n_exp), out_shap...  36.7 us
    pallas_call x1, Pallas kernels, local_step(): pl.pallas_call(adam_kernel, grid_spec=pltpu.PrefetchScalarGridSpec(num_sc...  5.04 us
    convert_element_type x1, other arithmetic, shards(): (serving_weights.astype(jnp.float32) + added).astype(jnp.bfloat16)  2.66 us
    unnamed x5, local copies, waits for them, and re-layouts  2.47 us

profile of v1, /device:TPU:0, one launch (start us, length us, event | category | flops | bytes accessed | tf_op | source)
XLA Modules:
  0.0 47.5 jit_solution(14936047147963104527)
XLA Ops:
  0.6 1.5 %copy.12 = s32[1,1,4,64,6]{4,3,2,1,0:T(8,128)} copy(s32[1,1,4,64,6]{3,2,4,1,0:T(4,128)} %param.12) | data formatting | bytes 12288 | tf_op args[4]
  2.1 5.0 %adam_step.1 = (f32[4,64,768]{2,1,0:T(8,128)}, f32[4,64,768]{2,1,0:T(8,128)}, f32[4,64,768]{2,1,0:T(8,128)}, bf16[4,64,768]{2,1,0:T(8,128)(2,1)}) custom-call(s32[4]{0:T(128)} %bitcast.17, s32[4]{0:T(128)} %owner_ref.1, f32[4,64,768]{2,1,0:T(8,128)} %bitcast.12, f32[4,64,768]{2,1,0:T(8,128)} %bitcast.13, f32[4,64,768]{2,1,0:T(8,128)} %bitcast.14, ...), custom_call_target="tpu_custom_call" | custom-call | tf_op jit(solution)/shard_map/adam_step/pallas_call | solution.py:47
  7.1 0.0 copy-start
  7.1 1.0 %copy-done = bf16[4,64,768]{2,1,0:T(8,128)(2,1)S(1)} copy-done((bf16[4,64,768]{2,1,0:T(8,128)(2,1)S(1)}, bf16[4,64,768]{2,1,0:T(8,128)(2,1)}, u32[]{:S(2)}) %copy-start) | copy-done | bytes 393240
  8.1 0.0 copy-start.1
  8.1 36.7 %exchange.1 = bf16[8,4,64,768]{3,2,1,0:T(8,128)(2,1)S(1)} custom-call(bf16[4,64,768]{2,1,0:T(8,128)(2,1)S(1)} %copy-done), custom_call_target="tpu_custom_call" | custom-call | bytes 3145728 | tf_op jit(solution)/shard_map/exchange/pallas_call | solution.py:148
  44.8 0.0 copy-done.1
  44.8 2.7 %fusion = bf16[1,2048,768]{2,1,0:T(8,128)(2,1)} fusion(bf16[1,2048,768]{2,1,0:T(8,128)(2,1)S(1)} %bitcast.11, bf16[1,2048,768]{2,1,0:T(8,128)(2,1)S(1)} %copy-done.1), kind=kLoop, calls=%fused_computation.1 | loop fusion | flops 6291456 | bytes 9437184 | tf_op jit(solution)/shard_map/convert_element_type | solution.py:200
Async XLA Ops:
  7.1 1.0 %copy-start = (bf16[4,64,768]{2,1,0:T(8,128)(2,1)S(1)}, bf16[4,64,768]{2,1,0:T(8,128)(2,1)}, u32[]{:S(2)}) copy-start(bf16[4,64,768]{2,1,0:T(8,128)(2,1)} %get-tuple-element.11.d_ref) | copy-start | bytes 1179652
  8.1 36.7 %copy-start.1 = (bf16[1,2048,768]{2,1,0:T(8,128)(2,1)S(1)}, bf16[1,2048,768]{2,1,0:T(8,128)(2,1)}, u32[]{:S(2)}) copy-start(bf16[1,2048,768]{2,1,0:T(8,128)(2,1)} %param.15) | copy-start | bytes 9437188

commit v2 on v1

v2 whole, which is shorter than its diff:
```python
import functools

import jax
import jax.numpy as jnp
from jax import lax
from jax.experimental import pallas as pl
from jax.experimental.pallas import tpu as pltpu
from jax.sharding import PartitionSpec as P

MESH = pl.DeviceIdType.MESH
CORES = 2


def adam(master, first_moment, second_moment, gradient):
    grad_full = gradient.astype(jnp.float32)
    first_out = 0.9 * first_moment + 0.1 * grad_full
    second_out = 0.95 * second_moment + 0.05 * grad_full * grad_full
    corr_first = 1.0 / (1.0 - 0.9**10)
    corr_second = 1.0 / (1.0 - 0.95**10)
    update = first_out * corr_first / (jnp.sqrt(second_out * corr_second) + 1e-08) + 0.1 * master
    delta = -0.1 * update
    return master + delta, first_out, second_out, delta


def adam_kernel(slot_ref, owner_ref, m_ref, f_ref, s_ref, g_ref, e_ref, mo_ref, fo_ref, so_ref, d_ref):
    columns = m_ref.shape[-1]
    blocks = e_ref.shape[0]
    width = columns // blocks
    exponent = e_ref[:, pl.ds(pl.program_id(0), 1), :][:, 0, :]
    limits = (jnp.left_shift(1, 7 - exponent).astype(jnp.float32) * (8.0 / 128.0)).T
    for b in range(blocks):
        cols = slice(b * width, (b + 1) * width)
        mo, fo, so, delta = adam(m_ref[0, :, cols], f_ref[0, :, cols], s_ref[0, :, cols], g_ref[0, :, cols])
        mo_ref[0, :, cols] = mo
        fo_ref[0, :, cols] = fo
        so_ref[0, :, cols] = so
        limit = limits[:, b : b + 1]
        d_ref[0, :, cols] = jnp.minimum(jnp.maximum(delta, -limit), limit).astype(jnp.bfloat16)


def local_step(slot_expert, expert_owner, master, first_moment, second_moment, gradient, scale_exponent):
    slots, rows, columns = master.shape
    by_block = jnp.transpose(scale_exponent, (2, 0, 1))
    here = pl.BlockSpec((1, rows, columns), lambda s, se, eo: (s, 0, 0))
    whole = pl.BlockSpec(by_block.shape, lambda s, se, eo: (0, 0, 0))
    owned = pl.BlockSpec((1, rows, columns), lambda s, se, eo: (eo[se[s]], 0, 0))
    flat = jax.ShapeDtypeStruct(master.shape, jnp.float32)
    return pl.pallas_call(
        adam_kernel,
        grid_spec=pltpu.PrefetchScalarGridSpec(
            num_scalar_prefetch=2,
            grid=(slots,),
            in_specs=[here, here, here, here, whole],
            out_specs=[here, here, here, owned],
        ),
        out_shape=[flat, flat, flat, jax.ShapeDtypeStruct(master.shape, jnp.bfloat16)],
        name="adam_step",
    )(slot_expert, expert_owner, master, first_moment, second_moment, gradient, by_block)


def ring_position(index, count):
    return (index // 2) * (1 - index % 2) + (count - 1 - index // 2) * (index % 2)


def ring_index(position, count):
    back = position // (count // 2)
    return 2 * position * (1 - back) + (2 * (count - 1 - position) + 1) * back


def exchange_kernel(
    n_rep, n_exp, d_ref, w_ref, out_ref, buf, weights, own_sem, w_sem, p_send, p_recv, r_send, r_recv
):
    rep = lax.axis_index("replica")
    exp = lax.axis_index("expert")
    pos = ring_position(rep, n_rep)
    ahead = ring_index((pos + 1) % n_rep, n_rep)
    behind = ring_index((pos + n_rep - 1) % n_rep, n_rep)
    chips = n_exp // CORES
    chip, core = exp // CORES, exp % CORES

    def peer(k, sign):
        dc, dk = k // CORES, k % CORES
        return ((chip + sign * dc + chips) % chips) * CORES + (core + sign * dk + CORES) % CORES

    barrier = pltpu.get_barrier_semaphore()
    for k in range(1, n_exp):
        pl.semaphore_signal(barrier, inc=1, device_id=(rep, peer(k, 1)), device_id_type=MESH)
    for near in (ahead, behind):
        pl.semaphore_signal(barrier, inc=1, device_id=(near, exp), device_id_type=MESH)
    own = pltpu.make_async_copy(d_ref.at[exp], buf.at[rep, exp], own_sem)
    own.start()
    load = pltpu.make_async_copy(w_ref, weights, w_sem)
    load.start()
    pl.semaphore_wait(barrier, n_exp + 1)

    far, near = n_rep // 2, n_rep - 1 - n_rep // 2
    hops = [[far if (k % 4 in (0, 3)) == (way == 0) else near for k in range(n_exp)] for way in (0, 1)]

    def origin(way, h):
        return ring_index((pos + n_rep - (h if way == 0 else n_rep - h)) % n_rep, n_rep)

    def ring(way, h, k):
        block = buf.at[origin(way, h), peer(k, -1)]
        return pltpu.make_async_remote_copy(
            src_ref=d_ref.at[exp] if h == 0 and k == 0 else block,
            dst_ref=block,
            send_sem=r_send.at[way, h, k],
            recv_sem=r_recv.at[way, h, k],
            device_id=(ahead if way == 0 else behind, exp),
            device_id_type=MESH,
        )

    def apply(source, k):
        at = (source, peer(k, -1))
        out_ref[at] = (weights[at].astype(jnp.float32) + buf[at].astype(jnp.float32)).astype(jnp.bfloat16)

    sent = []

    def forward(way, h, k):
        if h < hops[way][k]:
            copy = ring(way, h, k)
            copy.start()
            sent.append(copy)

    for way in (0, 1):
        forward(way, 0, 0)
    swaps = {}
    for k in list(range(CORES, n_exp)) + list(range(1, CORES)):
        swaps[k] = pltpu.make_async_remote_copy(
            src_ref=d_ref.at[peer(k, 1)],
            dst_ref=buf.at[rep, exp],
            send_sem=p_send.at[k],
            recv_sem=p_recv.at[k],
            device_id=(rep, peer(k, 1)),
            device_id_type=MESH,
        )
        swaps[k].start()

    for k in range(1, n_exp):
        swaps[k].wait_recv()
        for way in (0, 1):
            forward(way, 0, k)
    own.wait()
    load.wait()
    for k in range(n_exp):
        apply(rep, k)
    for h in range(1, far + 1):
        for k in range(n_exp):
            for way in (0, 1):
                if h <= hops[way][k]:
                    ring(way, h - 1, k).wait_recv()
                    forward(way, h, k)
                    apply(origin(way, h), k)
    for k in range(1, n_exp):
        swaps[k].wait_send()
    for copy in sent:
        copy.wait_send()


def exchange(n_rep, n_exp, delta, weights):
    slots, rows, columns = delta.shape
    whole = (n_rep, n_exp, rows, columns)
    size = n_rep * n_exp * rows * columns * 2
    far = n_rep // 2
    return pl.pallas_call(
        functools.partial(exchange_kernel, n_rep, n_exp),
        out_shape=jax.ShapeDtypeStruct(whole, jnp.bfloat16),
        in_specs=[pl.BlockSpec(memory_space=pltpu.HBM)] * 2,
        out_specs=pl.BlockSpec(memory_space=pltpu.VMEM),
        scratch_shapes=[
            pltpu.VMEM(whole, jnp.bfloat16),
            pltpu.VMEM(whole, jnp.bfloat16),
            pltpu.SemaphoreType.DMA(()),
            pltpu.SemaphoreType.DMA(()),
            pltpu.SemaphoreType.DMA((n_exp,)),
            pltpu.SemaphoreType.DMA((n_exp,)),
            pltpu.SemaphoreType.DMA((2, far, n_exp)),
            pltpu.SemaphoreType.DMA((2, far, n_exp)),
        ],
        compiler_params=pltpu.CompilerParams(
            collective_id=0, has_side_effects=True, vmem_limit_bytes=50 * 1024 * 1024
        ),
        cost_estimate=pl.CostEstimate(flops=0, bytes_accessed=3 * size, transcendentals=0),
        name="exchange",
    )(delta, weights.reshape(whole))


def exchange_by_collectives(delta):
    received = lax.all_to_all(delta, "expert", split_axis=0, concat_axis=0, tiled=True)
    return lax.all_gather(received, "replica", axis=0, tiled=False)


def shards(
    n_rep,
    n_exp,
    master,
    first_moment,
    second_moment,
    gradient,
    scale_exponent,
    slot_expert,
    expert_owner,
    serving_weights,
):
    master_out, first_out, second_out, delta = local_step(
        slot_expert[0, 0],
        expert_owner,
        master[0, 0],
        first_moment[0, 0],
        second_moment[0, 0],
        gradient[0, 0],
        scale_exponent[0, 0],
    )
    rows = master.shape[3]
    if rows % 16 == 0 and n_rep % 2 == 0 and n_exp % CORES == 0:
        serving_out = exchange(n_rep, n_exp, delta, serving_weights).reshape(serving_weights.shape)
    else:
        added = exchange_by_collectives(delta).reshape(serving_weights.shape).astype(jnp.float32)
        serving_out = (serving_weights.astype(jnp.float32) + added).astype(jnp.bfloat16)
    return (master_out[None, None], first_out[None, None], second_out[None, None], serving_out)


def solution(mesh):
    flat = P("replica", "expert", None, None, None)
    in_specs = (flat, flat, flat, flat, flat, P("replica", "expert", None), P(), P("expert", None, None))
    out_specs = (flat, flat, flat, P("expert", None, None))
    body = functools.partial(shards, mesh.shape["replica"], mesh.shape["expert"])
    return jax.shard_map(body, mesh=mesh, in_specs=in_specs, out_specs=out_specs, check_vma=False)
```

time: 47.8 us -> 45.4 us (0.950)
  other arithmetic: 2.66 us -> 0 us
    convert_element_type x1 -> x0, other arithmetic: 2.66 us -> none  [shards(): (serving_weights.astype(jnp.float32) + added).astype(jnp.bfloat16)]
    unnamed x5 -> x3, local copies, waits for them, and re-layouts: 2.47 us -> 2.66 us
where the time goes in v2:
time: 45.4 us; the launch traced here: 45.2 us
  Pallas kernels  41.9 us (92%)
  local copies, waits for them, and re-layouts  2.66 us (6%)
  between operations  0.64 us (1%)
    pallas_call x1, Pallas kernels, exchange(): pl.pallas_call(functools.partial(exchange_kernel, n_rep, n_exp), out_shap...  36.7 us
    pallas_call x1, Pallas kernels, local_step(): pl.pallas_call(adam_kernel, grid_spec=pltpu.PrefetchScalarGridSpec(num_sc...  5.21 us
    unnamed x3, local copies, waits for them, and re-layouts  2.66 us

profile of v2, /device:TPU:0, one launch (start us, length us, event | category | flops | bytes accessed | tf_op | source)
XLA Modules:
  0.0 45.2 jit_solution(13155768134265212530)
XLA Ops:
  0.6 5.2 %adam_step.1 = (f32[4,64,768]{2,1,0:T(8,128)}, f32[4,64,768]{2,1,0:T(8,128)}, f32[4,64,768]{2,1,0:T(8,128)}, bf16[4,64,768]{2,1,0:T(8,128)(2,1)}) custom-call(s32[4]{0:T(128)} %bitcast.20, s32[4]{0:T(128)} %owner_ref.1, f32[4,64,768]{2,1,0:T(8,128)} %bitcast.15, f32[4,64,768]{2,1,0:T(8,128)} %bitcast.16, f32[4,64,768]{2,1,0:T(8,128)} %bitcast.17, ...), custom_call_target="tpu_custom_call" | custom-call | tf_op jit(solution)/shard_map/adam_step/pallas_call | solution.py:48
  5.8 0.0 copy-start
  5.8 1.0 %copy-done = bf16[4,64,768]{2,1,0:T(8,128)(2,1)S(1)} copy-done((bf16[4,64,768]{2,1,0:T(8,128)(2,1)S(1)}, bf16[4,64,768]{2,1,0:T(8,128)(2,1)}, u32[]{:S(2)}) %copy-start) | copy-done | bytes 393240
  6.8 36.7 %exchange.1 = bf16[8,4,64,768]{3,2,1,0:T(8,128)(2,1)S(1)} custom-call(bf16[4,64,768]{2,1,0:T(8,128)(2,1)S(1)} %copy-done, bf16[8,4,64,768]{3,2,1,0:T(8,128)(2,1)} %bitcast.14), custom_call_target="tpu_custom_call" | custom-call | bytes 9437184 | tf_op jit(solution)/shard_map/exchange/pallas_call | solution.py:165
  43.5 1.7 %copy.13 = bf16[1,2048,768]{2,1,0:T(8,128)(2,1)} copy(bf16[1,2048,768]{2,1,0:T(8,128)(2,1)S(1)} %bitcast.13) | data formatting | bytes 6291456
Async XLA Ops:
  5.8 1.0 %copy-start = (bf16[4,64,768]{2,1,0:T(8,128)(2,1)S(1)}, bf16[4,64,768]{2,1,0:T(8,128)(2,1)}, u32[]{:S(2)}) copy-start(bf16[4,64,768]{2,1,0:T(8,128)(2,1)} %get-tuple-element.11.d_ref) | copy-start | bytes 1179652

commit v3 on v2

--- a/solution.py
+++ b/solution.py
@@ -67,8 +67,12 @@
     return 2 * position * (1 - back) + (2 * (count - 1 - position) + 1) * back
 
 
-def exchange_kernel(
-    n_rep, n_exp, d_ref, w_ref, out_ref, buf, weights, own_sem, w_sem, p_send, p_recv, r_send, r_recv
+def fused_kernel(
+    n_rep, n_exp,
+    slot_ref, owner_ref, m_ref, f_ref, s_ref, g_ref, e_ref, w_ref,
+    mo_ref, fo_ref, so_ref, out_ref,
+    m_in, f_in, s_in, g_in, e_in, m_new, f_new, s_new, d_buf, buf, weights, rows_new,
+    in_sem, w_sem, out_sem, rows_sem, p_send, p_recv, r_send, r_recv,
 ):
     rep = lax.axis_index("replica")
     exp = lax.axis_index("expert")
@@ -77,21 +81,50 @@
     behind = ring_index((pos + n_rep - 1) % n_rep, n_rep)
     chips = n_exp // CORES
     chip, core = exp // CORES, exp % CORES
+    columns = m_in.shape[-1]
+    blocks = e_in.shape[0]
+    width = columns // blocks
 
     def peer(k, sign):
         dc, dk = k // CORES, k % CORES
         return ((chip + sign * dc + chips) % chips) * CORES + (core + sign * dk + CORES) % CORES
 
+    pairs = ((m_ref, m_in), (f_ref, f_in), (s_ref, s_in), (g_ref, g_in), (e_ref, e_in))
+    loads = [pltpu.make_async_copy(src, dst, in_sem.at[i]) for i, (src, dst) in enumerate(pairs)]
+    for copy in loads:
+        copy.start()
     barrier = pltpu.get_barrier_semaphore()
     for k in range(1, n_exp):
         pl.semaphore_signal(barrier, inc=1, device_id=(rep, peer(k, 1)), device_id_type=MESH)
     for near in (ahead, behind):
         pl.semaphore_signal(barrier, inc=1, device_id=(near, exp), device_id_type=MESH)
-    own = pltpu.make_async_copy(d_ref.at[exp], buf.at[rep, exp], own_sem)
-    own.start()
+    for copy in loads:
+        copy.wait()
     load = pltpu.make_async_copy(w_ref, weights, w_sem)
     load.start()
-    pl.semaphore_wait(barrier, n_exp + 1)
+
+    def prepare(k):
+        target = peer(k, 1)
+        slot = 0
+        for i in range(n_exp):
+            slot = jnp.where(owner_ref[slot_ref[i]] == target, i, slot)
+        exponent = e_in[:, pl.ds(slot, 1), :][:, 0, :]
+        limits = (jnp.left_shift(1, 7 - exponent).astype(jnp.float32) * (8.0 / 128.0)).T
+        for b in range(blocks):
+            cols = slice(b * width, (b + 1) * width)
+            delta = adam(m_in[slot, :, cols], f_in[slot, :, cols], s_in[slot, :, cols], g_in[slot, :, cols])[3]
+            limit = limits[:, b : b + 1]
+            d_buf[k, :, cols] = jnp.minimum(jnp.maximum(delta, -limit), limit).astype(jnp.bfloat16)
+
+    def state(slot):
+        for b in range(blocks):
+            at = (slot, slice(None), slice(b * width, (b + 1) * width))
+            m_new[at], f_new[at], s_new[at], _ = adam(m_in[at], f_in[at], s_in[at], g_in[at])
+        for i, (src, dst) in enumerate(((m_new, mo_ref), (f_new, fo_ref), (s_new, so_ref))):
+            stored.append(pltpu.make_async_copy(src.at[slot], dst.at[slot], out_sem.at[i, slot]))
+            stored[-1].start()
+
+    stored = []
 
     far, near = n_rep // 2, n_rep - 1 - n_rep // 2
     hops = [[far if (k % 4 in (0, 3)) == (way == 0) else near for k in range(n_exp)] for way in (0, 1)]
@@ -102,7 +135,7 @@
     def ring(way, h, k):
         block = buf.at[origin(way, h), peer(k, -1)]
         return pltpu.make_async_remote_copy(
-            src_ref=d_ref.at[exp] if h == 0 and k == 0 else block,
+            src_ref=d_buf.at[0] if h == 0 and k == 0 else block,
             dst_ref=block,
             send_sem=r_send.at[way, h, k],
             recv_sem=r_recv.at[way, h, k],
@@ -110,9 +143,12 @@
             device_id_type=MESH,
         )
 
-    def apply(source, k):
+    def apply(source, k, step, own=False):
         at = (source, peer(k, -1))
-        out_ref[at] = (weights[at].astype(jnp.float32) + buf[at].astype(jnp.float32)).astype(jnp.bfloat16)
+        added = (d_buf[0] if own else buf[at]).astype(jnp.float32)
+        rows_new[at] = (weights[at].astype(jnp.float32) + added).astype(jnp.bfloat16)
+        stored.append(pltpu.make_async_copy(rows_new.at[at], out_ref.at[at], rows_sem.at[step, k]))
+        stored[-1].start()
 
     sent = []
 
@@ -122,12 +158,15 @@
             copy.start()
             sent.append(copy)
 
+    prepare(0)
+    pl.semaphore_wait(barrier, n_exp + 1)
     for way in (0, 1):
         forward(way, 0, 0)
     swaps = {}
-    for k in list(range(CORES, n_exp)) + list(range(1, CORES)):
+    for k in list(range(1, CORES)) + list(range(CORES, n_exp)):
+        prepare(k)
         swaps[k] = pltpu.make_async_remote_copy(
-            src_ref=d_ref.at[peer(k, 1)],
+            src_ref=d_buf.at[k],
             dst_ref=buf.at[rep, exp],
             send_sem=p_send.at[k],
             recv_sem=p_recv.at[k],
@@ -140,49 +179,66 @@
         swaps[k].wait_recv()
         for way in (0, 1):
             forward(way, 0, k)
-    own.wait()
+        state(k)
     load.wait()
+    state(0)
     for k in range(n_exp):
-        apply(rep, k)
+        apply(rep, k, 0, own=k == 0)
     for h in range(1, far + 1):
         for k in range(n_exp):
             for way in (0, 1):
                 if h <= hops[way][k]:
                     ring(way, h - 1, k).wait_recv()
                     forward(way, h, k)
-                    apply(origin(way, h), k)
+                    apply(origin(way, h), k, 2 * h - 1 + way)
     for k in range(1, n_exp):
         swaps[k].wait_send()
     for copy in sent:
         copy.wait_send()
-
-
-def exchange(n_rep, n_exp, delta, weights):
-    slots, rows, columns = delta.shape
+    for copy in stored:
+        copy.wait()
+
+
+def fused(n_rep, n_exp, slot_expert, expert_owner, master, first, second, gradient, scale_exponent, weights):
+    slots, rows, columns = master.shape
+    by_block = jnp.transpose(scale_exponent, (2, 0, 1))
     whole = (n_rep, n_exp, rows, columns)
     size = n_rep * n_exp * rows * columns * 2
     far = n_rep // 2
+    flat = jax.ShapeDtypeStruct(master.shape, jnp.float32)
     return pl.pallas_call(
-        functools.partial(exchange_kernel, n_rep, n_exp),
-        out_shape=jax.ShapeDtypeStruct(whole, jnp.bfloat16),
-        in_specs=[pl.BlockSpec(memory_space=pltpu.HBM)] * 2,
-        out_specs=pl.BlockSpec(memory_space=pltpu.VMEM),
+        functools.partial(fused_kernel, n_rep, n_exp),
+        out_shape=[flat, flat, flat, jax.ShapeDtypeStruct(whole, jnp.bfloat16)],
+        in_specs=[pl.BlockSpec(memory_space=pltpu.SMEM)] * 2 + [pl.BlockSpec(memory_space=pl.ANY)] * 6,
+        out_specs=[pl.BlockSpec(memory_space=pl.ANY)] * 4,
         scratch_shapes=[
+            pltpu.VMEM(master.shape, jnp.float32),
+            pltpu.VMEM(master.shape, jnp.float32),
+            pltpu.VMEM(master.shape, jnp.float32),
+            pltpu.VMEM(master.shape, jnp.bfloat16),
+            pltpu.VMEM(by_block.shape, jnp.int32),
+            pltpu.VMEM(master.shape, jnp.float32),
+            pltpu.VMEM(master.shape, jnp.float32),
+            pltpu.VMEM(master.shape, jnp.float32),
+            pltpu.VMEM(master.shape, jnp.bfloat16),
             pltpu.VMEM(whole, jnp.bfloat16),
             pltpu.VMEM(whole, jnp.bfloat16),
+            pltpu.VMEM(whole, jnp.bfloat16),
+            pltpu.SemaphoreType.DMA((5,)),
             pltpu.SemaphoreType.DMA(()),
-            pltpu.SemaphoreType.DMA(()),
+            pltpu.SemaphoreType.DMA((3, slots)),
+            pltpu.SemaphoreType.DMA((2 * far + 1, n_exp)),
             pltpu.SemaphoreType.DMA((n_exp,)),
             pltpu.SemaphoreType.DMA((n_exp,)),
             pltpu.SemaphoreType.DMA((2, far, n_exp)),
             pltpu.SemaphoreType.DMA((2, far, n_exp)),
         ],
         compiler_params=pltpu.CompilerParams(
-            collective_id=0, has_side_effects=True, vmem_limit_bytes=50 * 1024 * 1024
+            collective_id=0, has_side_effects=True, vmem_limit_bytes=60 * 1024 * 1024
         ),
         cost_estimate=pl.CostEstimate(flops=0, bytes_accessed=3 * size, transcendentals=0),
-        name="exchange",
-    )(delta, weights.reshape(whole))
+        name="fused_step",
+    )(slot_expert, expert_owner, master, first, second, gradient, by_block, weights.reshape(whole))
 
 
 def exchange_by_collectives(delta):
@@ -202,7 +258,7 @@
     expert_owner,
     serving_weights,
 ):
-    master_out, first_out, second_out, delta = local_step(
+    state = (
         slot_expert[0, 0],
         expert_owner,
         master[0, 0],
@@ -213,8 +269,10 @@
     )
     rows = master.shape[3]
     if rows % 16 == 0 and n_rep % 2 == 0 and n_exp % CORES == 0:
-        serving_out = exchange(n_rep, n_exp, delta, serving_weights).reshape(serving_weights.shape)
+        master_out, first_out, second_out, new_rows = fused(n_rep, n_exp, *state, serving_weights)
+        serving_out = new_rows.reshape(serving_weights.shape)
     else:
+        master_out, first_out, second_out, delta = local_step(*state)
         added = exchange_by_collectives(delta).reshape(serving_weights.shape).astype(jnp.float32)
         serving_out = (serving_weights.astype(jnp.float32) + added).astype(jnp.bfloat16)
     return (master_out[None, None], first_out[None, None], second_out[None, None], serving_out)

time: 45.4 us -> 48.5 us (1.068)
  local copies, waits for them, and re-layouts: 2.66 us -> 8.07 us
  Pallas kernels: 41.9 us -> 39.6 us
    unnamed x3 -> x6, local copies, waits for them, and re-layouts: 2.66 us -> 8.07 us
    pallas_call x2 -> x1, Pallas kernels: 41.9 us -> 39.6 us  [fused(): pl.pallas_call(functools.partial(fused_kernel, n_rep, n_exp), out_shape=[...]
where the time goes in v3:
time: 48.5 us; the launch traced here: 48.3 us
  Pallas kernels  39.6 us (82%)
  local copies, waits for them, and re-layouts  8.07 us (17%)
  between operations  0.65 us (1%)
    pallas_call x1, Pallas kernels, fused(): pl.pallas_call(functools.partial(fused_kernel, n_rep, n_exp), out_shape=[...  39.6 us
    unnamed x6, local copies, waits for them, and re-layouts  8.07 us

profile of v3, /device:TPU:0, one launch (start us, length us, event | category | flops | bytes accessed | tf_op | source)
XLA Modules:
  0.0 48.3 jit_solution(14870352830489843839)
XLA Ops:
  0.6 39.6 %fused_step.1 = (f32[4,64,768]{2,1,0:T(8,128)}, f32[4,64,768]{2,1,0:T(8,128)}, f32[4,64,768]{2,1,0:T(8,128)}, bf16[8,4,64,768]{3,2,1,0:T(8,128)(2,1)}) custom-call(s32[4]{0:T(128)} %bitcast.23, s32[4]{0:T(128)} %owner_ref.1, f32[4,64,768]{2,1,0:T(8,128)} %bitcast.18, f32[4,64,768]{2,1,0:T(8,128)} %bitcast.19, f32[4,64,768]{2,1,0:T(8,128)} %bitcast.20, ...), custom_call_target="tpu_custom_call" | custom-call | bytes 9437184 | tf_op jit(solution)/shard_map/fused_step/pallas_call | solution.py:209
  40.2 0.0 copy-start
  40.2 2.2 %copy.16 = f32[1,1,4,64,768]{4,3,2,1,0:T(8,128)} copy(f32[1,1,4,64,768]{4,3,2,1,0:T(8,128)} %bitcast.17) | data formatting | bytes 1572864
  42.5 2.1 %copy.17 = f32[1,1,4,64,768]{4,3,2,1,0:T(8,128)} copy(f32[1,1,4,64,768]{4,3,2,1,0:T(8,128)} %bitcast.16) | data formatting | bytes 1572864
  44.5 2.1 %copy.18 = f32[1,1,4,64,768]{4,3,2,1,0:T(8,128)} copy(f32[1,1,4,64,768]{4,3,2,1,0:T(8,128)} %bitcast.15) | data formatting | bytes 1572864
  46.6 0.0 copy-done
  46.6 1.7 %copy.19 = bf16[1,2048,768]{2,1,0:T(8,128)(2,1)} copy(bf16[1,2048,768]{2,1,0:T(8,128)(2,1)S(1)} %bitcast.13) | data formatting | bytes 6291456
Async XLA Ops:
  40.2 6.4 %copy-start = (bf16[8,4,64,768]{3,2,1,0:T(8,128)(2,1)S(1)}, bf16[8,4,64,768]{3,2,1,0:T(8,128)(2,1)}, u32[]{:S(2)}) copy-start(bf16[8,4,64,768]{3,2,1,0:T(8,128)(2,1)} %get-tuple-element.11) | copy-start | bytes 9437188

commit v4 on v2

--- a/solution.py
+++ b/solution.py
@@ -22,38 +22,67 @@
     return master + delta, first_out, second_out, delta
 
 
-def adam_kernel(slot_ref, owner_ref, m_ref, f_ref, s_ref, g_ref, e_ref, mo_ref, fo_ref, so_ref, d_ref):
-    columns = m_ref.shape[-1]
-    blocks = e_ref.shape[0]
+def adam_kernel(
+    slot_ref, owner_ref, m_ref, f_ref, s_ref, g_ref, e_ref, mo_ref, fo_ref, so_ref, d_ref,
+    m_in, f_in, s_in, g_in, e_in, m_new, f_new, s_new, e_sem, in_sem, out_sem,
+):
+    slots, _, columns = m_in.shape
+    blocks = e_in.shape[0]
     width = columns // blocks
-    exponent = e_ref[:, pl.ds(pl.program_id(0), 1), :][:, 0, :]
-    limits = (jnp.left_shift(1, 7 - exponent).astype(jnp.float32) * (8.0 / 128.0)).T
-    for b in range(blocks):
-        cols = slice(b * width, (b + 1) * width)
-        mo, fo, so, delta = adam(m_ref[0, :, cols], f_ref[0, :, cols], s_ref[0, :, cols], g_ref[0, :, cols])
-        mo_ref[0, :, cols] = mo
-        fo_ref[0, :, cols] = fo
-        so_ref[0, :, cols] = so
-        limit = limits[:, b : b + 1]
-        d_ref[0, :, cols] = jnp.minimum(jnp.maximum(delta, -limit), limit).astype(jnp.bfloat16)
+    exponents = pltpu.make_async_copy(e_ref, e_in, e_sem)
+    exponents.start()
+    pairs = ((m_ref, m_in), (f_ref, f_in), (s_ref, s_in), (g_ref, g_in))
+    loads = [
+        [pltpu.make_async_copy(src.at[s], dst.at[s], in_sem.at[i, s]) for i, (src, dst) in enumerate(pairs)]
+        for s in range(slots)
+    ]
+    for copies in loads:
+        for copy in copies:
+            copy.start()
+    exponents.wait()
+    stores = []
+    for s, copies in enumerate(loads):
+        target = owner_ref[slot_ref[s]]
+        limits = (jnp.left_shift(1, 7 - e_in[:, s, :]).astype(jnp.float32) * (8.0 / 128.0)).T
+        for copy in copies:
+            copy.wait()
+        for b in range(blocks):
+            cols = slice(b * width, (b + 1) * width)
+            at = (s, slice(None), cols)
+            m_new[at], f_new[at], s_new[at], delta = adam(m_in[at], f_in[at], s_in[at], g_in[at])
+            limit = limits[:, b : b + 1]
+            d_ref[target, :, cols] = jnp.minimum(jnp.maximum(delta, -limit), limit).astype(jnp.bfloat16)
+        for i, (src, dst) in enumerate(((m_new, mo_ref), (f_new, fo_ref), (s_new, so_ref))):
+            stores.append(pltpu.make_async_copy(src.at[s], dst.at[s], out_sem.at[i, s]))
+            stores[-1].start()
+    for copy in stores:
+        copy.wait()
 
 
 def local_step(slot_expert, expert_owner, master, first_moment, second_moment, gradient, scale_exponent):
-    slots, rows, columns = master.shape
+    slots = master.shape[0]
     by_block = jnp.transpose(scale_exponent, (2, 0, 1))
-    here = pl.BlockSpec((1, rows, columns), lambda s, se, eo: (s, 0, 0))
-    whole = pl.BlockSpec(by_block.shape, lambda s, se, eo: (0, 0, 0))
-    owned = pl.BlockSpec((1, rows, columns), lambda s, se, eo: (eo[se[s]], 0, 0))
     flat = jax.ShapeDtypeStruct(master.shape, jnp.float32)
+    held = pltpu.VMEM(master.shape, jnp.float32)
     return pl.pallas_call(
         adam_kernel,
-        grid_spec=pltpu.PrefetchScalarGridSpec(
-            num_scalar_prefetch=2,
-            grid=(slots,),
-            in_specs=[here, here, here, here, whole],
-            out_specs=[here, here, here, owned],
-        ),
+        in_specs=[pl.BlockSpec(memory_space=pltpu.SMEM)] * 2 + [pl.BlockSpec(memory_space=pl.ANY)] * 5,
+        out_specs=[pl.BlockSpec(memory_space=pl.ANY)] * 3 + [pl.BlockSpec(memory_space=pltpu.VMEM)],
         out_shape=[flat, flat, flat, jax.ShapeDtypeStruct(master.shape, jnp.bfloat16)],
+        scratch_shapes=[
+            held,
+            held,
+            held,
+            pltpu.VMEM(master.shape, jnp.bfloat16),
+            pltpu.VMEM(by_block.shape, jnp.int32),
+            held,
+            held,
+            held,
+            pltpu.SemaphoreType.DMA(()),
+            pltpu.SemaphoreType.DMA((4, slots)),
+            pltpu.SemaphoreType.DMA((3, slots)),
+        ],
+        compiler_params=pltpu.CompilerParams(vmem_limit_bytes=107 * 512 * 1024),
         name="adam_step",
     )(slot_expert, expert_owner, master, first_moment, second_moment, gradient, by_block)
 

time: 45.4 us -> 45 us (level)
  Pallas kernels: 41.9 us -> 40.4 us
  local copies, waits for them, and re-layouts: 2.66 us -> 3.68 us
    pallas_call x1, Pallas kernels: 5.21 us -> 3.65 us  [local_step(): pl.pallas_call(adam_kernel, in_specs=[pl.BlockSpec(memory_space=pltpu.SME...]
    unnamed x3 -> x7, local copies, waits for them, and re-layouts: 2.66 us -> 3.68 us
where the time goes in v4:
time: 45 us; the launch traced here: 44.8 us
  Pallas kernels  40.4 us (90%)
  local copies, waits for them, and re-layouts  3.68 us (8%)
  between operations  0.66 us (1%)
    pallas_call x1, Pallas kernels, exchange(): pl.pallas_call(functools.partial(exchange_kernel, n_rep, n_exp), out_shap...  36.8 us
    unnamed x7, local copies, waits for them, and re-layouts  3.68 us
    pallas_call x1, Pallas kernels, local_step(): pl.pallas_call(adam_kernel, in_specs=[pl.BlockSpec(memory_space=pltpu.SME...  3.65 us

profile of v4, /device:TPU:0, one launch (start us, length us, event | category | flops | bytes accessed | tf_op | source)
XLA Modules:
  0.0 44.8 jit_solution(8527431418865991241)
XLA Ops:
  0.6 0.0 copy-start
  0.6 0.7 %copy-done = s32[1,1,4,64,6]{3,2,4,1,0:T(4,128)S(1)} copy-done((s32[1,1,4,64,6]{3,2,4,1,0:T(4,128)S(1)}, s32[1,1,4,64,6]{3,2,4,1,0:T(4,128)}, u32[]{:S(2)}) %copy-start) | copy-done | bytes 6168
  1.3 0.0 copy-start.1
  1.3 0.7 %copy-done.1 = s32[1,1,4]{2,1,0:T(1,128)S(1)} copy-done((s32[1,1,4]{2,1,0:T(1,128)S(1)}, s32[1,1,4]{2,1,0:T(1,128)}, u32[]{:S(2)}) %copy-start.1) | copy-done | bytes 40
  2.0 0.0 copy-start.2
  2.0 0.7 %copy-done.2 = s32[4]{0:T(128)S(1)} copy-done((s32[4]{0:T(128)S(1)}, s32[4]{0:T(128)}, u32[]{:S(2)}) %copy-start.2) | copy-done | bytes 40
  2.7 3.7 %adam_step.1 = (f32[4,64,768]{2,1,0:T(8,128)}, f32[4,64,768]{2,1,0:T(8,128)}, f32[4,64,768]{2,1,0:T(8,128)}, bf16[4,64,768]{2,1,0:T(8,128)(2,1)S(1)}) custom-call(s32[4]{0:T(128)S(1)} %bitcast.15, s32[4]{0:T(128)S(1)} %copy-done.2, f32[4,64,768]{2,1,0:T(8,128)} %bitcast.17, f32[4,64,768]{2,1,0:T(8,128)} %bitcast.18, f32[4,64,768]{2,1,0:T(8,128)} %bitcast.19, ...), custom_call_target="tpu_custom_call" | custom-call | tf_op jit(solution)/shard_map/adam_step/pallas_call | solution.py:67
  6.3 36.8 %exchange.1 = bf16[8,4,64,768]{3,2,1,0:T(8,128)(2,1)S(1)} custom-call(bf16[4,64,768]{2,1,0:T(8,128)(2,1)S(1)} %get-tuple-element.11.d_ref, bf16[8,4,64,768]{3,2,1,0:T(8,128)(2,1)} %bitcast.16), custom_call_target="tpu_custom_call" | custom-call | bytes 9437184 | tf_op jit(solution)/shard_map/exchange/pallas_call | solution.py:194
  43.1 1.7 %copy.13 = bf16[1,2048,768]{2,1,0:T(8,128)(2,1)} copy(bf16[1,2048,768]{2,1,0:T(8,128)(2,1)S(1)} %bitcast.13) | data formatting | bytes 6291456
Async XLA Ops:
  0.6 0.7 %copy-start = (s32[1,1,4,64,6]{3,2,4,1,0:T(4,128)S(1)}, s32[1,1,4,64,6]{3,2,4,1,0:T(4,128)}, u32[]{:S(2)}) copy-start(s32[1,1,4,64,6]{3,2,4,1,0:T(4,128)} %param.12) | copy-start | bytes 18436
  1.3 0.7 %copy-start.1 = (s32[1,1,4]{2,1,0:T(1,128)S(1)}, s32[1,1,4]{2,1,0:T(1,128)}, u32[]{:S(2)}) copy-start(s32[1,1,4]{2,1,0:T(1,128)} %param.13) | copy-start | bytes 52
  2.0 0.7 %copy-start.2 = (s32[4]{0:T(128)S(1)}, s32[4]{0:T(128)}, u32[]{:S(2)}) copy-start(s32[4]{0:T(128)} %owner_ref.1) | copy-start | bytes 52

commit v5 on v4

--- a/solution.py
+++ b/solution.py
@@ -82,7 +82,7 @@
             pltpu.SemaphoreType.DMA((4, slots)),
             pltpu.SemaphoreType.DMA((3, slots)),
         ],
-        compiler_params=pltpu.CompilerParams(vmem_limit_bytes=107 * 512 * 1024),
+        compiler_params=pltpu.CompilerParams(vmem_limit_bytes=118 * 512 * 1024),
         name="adam_step",
     )(slot_expert, expert_owner, master, first_moment, second_moment, gradient, by_block)
 

time: 45 us -> 45.2 us (level)
  Pallas kernels: 40.4 us -> 41.7 us
  local copies, waits for them, and re-layouts: 3.68 us -> 2.66 us
    pallas_call x1, Pallas kernels: 3.65 us -> 5.03 us  [local_step(): pl.pallas_call(adam_kernel, in_specs=[pl.BlockSpec(memory_space=pltpu.SME...]
    unnamed x7 -> x3, local copies, waits for them, and re-layouts: 3.68 us -> 2.66 us
where the time goes in v5:
time: 45.2 us; the launch traced here: 45 us
  Pallas kernels  41.7 us (92%)
  local copies, waits for them, and re-layouts  2.66 us (6%)
  between operations  0.66 us (1%)
    pallas_call x1, Pallas kernels, exchange(): pl.pallas_call(functools.partial(exchange_kernel, n_rep, n_exp), out_shap...  36.7 us
    pallas_call x1, Pallas kernels, local_step(): pl.pallas_call(adam_kernel, in_specs=[pl.BlockSpec(memory_space=pltpu.SME...  5.03 us
    unnamed x3, local copies, waits for them, and re-layouts  2.66 us

profile of v5, /device:TPU:0, one launch (start us, length us, event | category | flops | bytes accessed | tf_op | source)
XLA Modules:
  0.0 45.0 jit_solution(5499781834108435107)
XLA Ops:
  0.6 5.0 %adam_step.1 = (f32[4,64,768]{2,1,0:T(8,128)}, f32[4,64,768]{2,1,0:T(8,128)}, f32[4,64,768]{2,1,0:T(8,128)}, bf16[4,64,768]{2,1,0:T(8,128)(2,1)}) custom-call(s32[4]{0:T(128)} %bitcast.20, s32[4]{0:T(128)} %owner_ref.1, f32[4,64,768]{2,1,0:T(8,128)} %bitcast.15, f32[4,64,768]{2,1,0:T(8,128)} %bitcast.16, f32[4,64,768]{2,1,0:T(8,128)} %bitcast.17, ...), custom_call_target="tpu_custom_call" | custom-call | tf_op jit(solution)/shard_map/adam_step/pallas_call | solution.py:67
  5.7 0.0 copy-start
  5.7 1.0 %copy-done = bf16[4,64,768]{2,1,0:T(8,128)(2,1)S(1)} copy-done((bf16[4,64,768]{2,1,0:T(8,128)(2,1)S(1)}, bf16[4,64,768]{2,1,0:T(8,128)(2,1)}, u32[]{:S(2)}) %copy-start) | copy-done | bytes 393240
  6.7 36.7 %exchange.1 = bf16[8,4,64,768]{3,2,1,0:T(8,128)(2,1)S(1)} custom-call(bf16[4,64,768]{2,1,0:T(8,128)(2,1)S(1)} %copy-done, bf16[8,4,64,768]{3,2,1,0:T(8,128)(2,1)} %bitcast.14), custom_call_target="tpu_custom_call" | custom-call | bytes 9437184 | tf_op jit(solution)/shard_map/exchange/pallas_call | solution.py:194
  43.4 1.7 %copy.13 = bf16[1,2048,768]{2,1,0:T(8,128)(2,1)} copy(bf16[1,2048,768]{2,1,0:T(8,128)(2,1)S(1)} %bitcast.13) | data formatting | bytes 6291456
Async XLA Ops:
  5.7 1.0 %copy-start = (bf16[4,64,768]{2,1,0:T(8,128)(2,1)S(1)}, bf16[4,64,768]{2,1,0:T(8,128)(2,1)}, u32[]{:S(2)}) copy-start(bf16[4,64,768]{2,1,0:T(8,128)(2,1)} %get-tuple-element.11.d_ref) | copy-start | bytes 1179652
